TPU v7x, 128 devices: a whole 4x4x4 slice. The times are simulated.
128 devices in a mesh: enc: 4 (over z), region: 32 (over y, x, core).
Axes of the slice: x: 4, y: 4, z: 4, core: 2. Of those that a mesh axis runs over, the one named last changes fastest.
Arguments:
- embeddings: bfloat16 [131072, 1536], P(('enc', 'region')), may hold values from -6 to 6
- tile_position: int32 [131072], P(('enc', 'region')), may hold values from 0 to 131071, as said below
- w_in: bfloat16 [1536, 768], replicated, may hold values from -0.15625 to 0.15625
- ln_gain: bfloat16 [768], replicated, may hold values from 0.099609375 to 1.8984375
- w_query: bfloat16 [768, 768], replicated, may hold values from -0.14505926 to 0.14505926
- w_key: bfloat16 [768, 768], replicated, may hold values from -1.8222618 to 1.8222618
- w_value: bfloat16 [768, 768], replicated, may hold values from -0.21875 to 0.21875
- w_out: bfloat16 [768, 768], replicated, may hold values from -0.21875 to 0.21875
- near_lengths: int32 [4, 256], replicated, may hold values from 1 to 256, 32768 in all within a row
- far_lengths: int32 [4, 64], replicated, may hold values from 1 to 1024, 32768 in all within a row
- tissue: int32 [131072], P(('enc', 'region')), may hold values 0 or 1
- hospital: int32 [4], replicated, may hold values from 0 to 1, as said below
- w_kernel: float32 [768, 256], replicated, may hold values from -0.21875 to 0.21875
Outputs:
- features: bfloat16 [131072, 768], P(('enc', 'region'))
- statistic: float32 [], replicated
- kernel_grad: float32 [768, 256], replicated
Inputs may be any that keep to these rules, and one draw needn't show every extreme that they name: `tile_position`: every number of 0 to 131071 appears once; the 1024 rows of each device hold exactly 8 positions of each device's block of 1024 consecutive tile positions. `hospital`: each of the two labels is held by at least one of the 4 slides.
All inputs are finite; a program needn't handle non-finite values. No bound on the sum of `tissue` on one device may be relied on, other than what follows from the above.
Results may differ from a plain program's by a relative error of at most 0.012.
Values may be sent and summed in bfloat16 or wider, within the bound.
A program may use at most 128 MiB of HBM per device.

v0:
```python
import jax
import jax.numpy as jnp
from jax import lax
from jax.sharding import PartitionSpec as P

HEADS = 16
REGION = 256
DILATION = 4
NORM_EPSILON = 1e-05
MASKED_SCORE = -1e30
GRAD_SCALE = 100.0


def with_halo(x, sides, width):
    for axis, dim in sides:
        devices, length = (lax.axis_size(axis), x.shape[dim])
        up = [(i, (i + 1) % devices) for i in range(devices - 1)]
        down = [(j, i) for i, j in up]
        last = lax.slice_in_dim(x, length - width, length, axis=dim)
        initial = lax.slice_in_dim(x, 0, width, axis=dim)
        before = lax.ppermute(last, axis, up)
        after = lax.ppermute(initial, axis, down)
        x = jnp.concatenate([before, x, after], axis=dim)
    return x


def layer_norm(inputs):
    center = inputs - jnp.mean(inputs, axis=-1, keepdims=True)
    spread = jnp.mean(center * center, axis=-1, keepdims=True)
    return center * lax.rsqrt(spread + NORM_EPSILON)


def segment_ids(positions, lengths):
    segment_ends = jnp.cumsum(lengths, dtype=jnp.int32)
    passed = (segment_ends <= positions[..., None]).astype(jnp.int32)
    return jnp.sum(passed, axis=-1, dtype=jnp.int32)


def attend(queries, key_rows, values, key_pos, query_seg, key_seg, slide_len):
    scaling = queries.shape[-1] ** (-0.5)
    scores = (
        jnp.einsum("bqhe,bkhe->bhqk", queries, key_rows, preferred_element_type=jnp.float32)
        * scaling
    )
    allowed = (
        (query_seg[:, :, None] == key_seg[:, None, :])
        & (key_pos[:, None, :] >= 0)
        & (key_pos[:, None, :] < slide_len)
    )
    allowed = allowed[:, None, :, :]
    masked = jnp.where(allowed, scores, MASKED_SCORE)
    row_peak = jnp.max(masked, axis=-1, keepdims=True)
    exponent = jnp.where(allowed, jnp.exp(masked - row_peak), 0.0)
    row_total = jnp.sum(exponent, axis=-1, keepdims=True)
    weights = (exponent / row_total).astype(jnp.bfloat16)
    context = jnp.einsum("bhqk,bkhe->bqhe", weights, values, preferred_element_type=jnp.float32)
    return context.astype(jnp.bfloat16)


def block_context(queries, near_kv, far_kv, base_pos, near_row, far_row, slide_len):
    tile_rows, width = queries.shape
    half_width = width // 2
    head_count = HEADS // 2
    head_size = width // HEADS
    near_span = tile_rows // 4
    half_rows = tile_rows // 2
    steps_near = jnp.arange(tile_rows, dtype=jnp.int32)
    near_query = queries[:, :half_width].reshape(2, half_rows, head_count, head_size)
    near_keys = jnp.stack(
        [near_kv[0, :tile_rows], near_kv[0, half_rows : half_rows + tile_rows]]
    ).reshape(2, tile_rows, head_count, head_size)
    near_values = jnp.stack(
        [near_kv[1, :tile_rows], near_kv[1, half_rows : half_rows + tile_rows]]
    ).reshape(2, tile_rows, head_count, head_size)
    query_pos = base_pos + steps_near.reshape(2, half_rows)
    key_pos = base_pos - near_span + jnp.stack([steps_near, steps_near + half_rows])
    near_context = attend(
        near_query,
        near_keys,
        near_values,
        key_pos,
        segment_ids(query_pos, near_row),
        segment_ids(key_pos, near_row),
        slide_len,
    )
    near_context = near_context.reshape(tile_rows, half_width)
    group_rows = tile_rows // DILATION
    far_query = (
        queries[:, half_width:]
        .reshape(group_rows, DILATION, head_count, head_size)
        .transpose(1, 0, 2, 3)
    )
    far_keys = (
        far_kv[0].reshape(3 * group_rows, DILATION, head_count, head_size).transpose(1, 0, 2, 3)
    )
    far_values = (
        far_kv[1].reshape(3 * group_rows, DILATION, head_count, head_size).transpose(1, 0, 2, 3)
    )
    offsets = jnp.arange(DILATION, dtype=jnp.int32)[:, None]
    far_query_pos = base_pos + DILATION * jnp.arange(group_rows, dtype=jnp.int32)[None, :] + offsets
    far_key_pos = (
        base_pos
        - tile_rows
        + DILATION * jnp.arange(3 * group_rows, dtype=jnp.int32)[None, :]
        + offsets
    )
    far_context = attend(
        far_query,
        far_keys,
        far_values,
        far_key_pos,
        segment_ids(far_query_pos, far_row),
        segment_ids(far_key_pos, far_row),
        slide_len,
    )
    far_context = far_context.transpose(1, 0, 2, 3).reshape(tile_rows, half_width)
    return jnp.concatenate([near_context, far_context], axis=1)


def gaussian(left, right):
    left_sq = jnp.sum(left * left, axis=1)
    right_sq = jnp.sum(right * right, axis=1)
    inner = jnp.dot(left, right.T, precision=lax.Precision.HIGHEST)
    return jnp.exp(-(left_sq[:, None] + right_sq[None, :] - 2.0 * inner) / (2.0 * left.shape[1]))


def local(
    embeddings,
    tile_position,
    w_in,
    ln_gain,
    w_query,
    w_key,
    w_value,
    w_out,
    near_lengths,
    far_lengths,
    tissue,
    hospital,
    w_kernel,
):
    tile_rows = embeddings.shape[0]
    enc_count = lax.axis_size("enc")
    region_count = lax.axis_size("region")
    senders = enc_count * region_count
    per_peer = tile_rows // senders
    outgoing = jnp.argsort(tile_position)
    sorted_pos = tile_position[outgoing]
    payload = embeddings[outgoing]
    width_sent = payload.shape[1]
    arrived, arrived_pos = (
        lax.all_to_all(
            payload.reshape(senders, per_peer, width_sent),
            ("enc", "region"),
            split_axis=0,
            concat_axis=0,
            tiled=True,
        ),
        lax.all_to_all(
            sorted_pos.reshape(senders, per_peer),
            ("enc", "region"),
            split_axis=0,
            concat_axis=0,
            tiled=True,
        ),
    )
    placing = jnp.argsort(arrived_pos.reshape(tile_rows) % tile_rows)
    landed = arrived.reshape(tile_rows, width_sent)[placing]
    start_rows = jnp.dot(landed, w_in, preferred_element_type=jnp.float32).astype(jnp.bfloat16)
    normed = (layer_norm(start_rows.astype(jnp.float32)) * ln_gain.astype(jnp.float32)).astype(
        jnp.bfloat16
    )
    queries = jnp.dot(normed, w_query, preferred_element_type=jnp.float32).astype(jnp.bfloat16)
    d_model = queries.shape[1]
    half_width = d_model // 2
    near_span = tile_rows // 4
    base_pos = lax.axis_index("region") * tile_rows
    slide_len = tile_rows * region_count
    near_own = jnp.einsum(
        "rd,sdc->src",
        normed,
        jnp.stack([w_key[:, :half_width], w_value[:, :half_width]]),
        preferred_element_type=jnp.float32,
    ).astype(jnp.bfloat16)
    far_own = jnp.einsum(
        "rd,sdc->src",
        normed,
        jnp.stack([w_key[:, half_width:], w_value[:, half_width:]]),
        preferred_element_type=jnp.float32,
    ).astype(jnp.bfloat16)
    near_kv = with_halo(near_own, (("region", 1),), near_span)
    far_kv = with_halo(far_own, (("region", 1),), tile_rows)
    slide_index = lax.axis_index("enc")
    near_row = lax.dynamic_index_in_dim(near_lengths, slide_index, 0, keepdims=False)
    far_row = lax.dynamic_index_in_dim(far_lengths, slide_index, 0, keepdims=False)
    context = block_context(queries, near_kv, far_kv, base_pos, near_row, far_row, slide_len)
    features = (
        start_rows.astype(jnp.float32) + jnp.dot(context, w_out, preferred_element_type=jnp.float32)
    ).astype(jnp.bfloat16)
    reg_dev = tile_rows // REGION
    per_slide = reg_dev * region_count
    region_total = reg_dev * senders
    pooled = (
        jnp.einsum(
            "grd,gr->gd",
            features.reshape(reg_dev, REGION, d_model),
            tissue.reshape(reg_dev, REGION).astype(jnp.bfloat16),
            preferred_element_type=jnp.float32,
        )
        / REGION
    )
    normal_pool = layer_norm(pooled)
    slide_ids = jnp.arange(hospital.shape[0], dtype=jnp.int32)
    labelled_one = jnp.sum(hospital).astype(jnp.float32)
    count_one = labelled_one * per_slide
    count_zero = (hospital.shape[0] - labelled_one) * per_slide

    def region_weights(region_ids):
        owner_slide = region_ids // per_slide
        label_of = jnp.sum(
            jnp.where(owner_slide[:, None] == slide_ids[None, :], hospital[None, :], 0), axis=1
        )
        return jnp.where(label_of == 1, 1.0 / count_one, -1.0 / count_zero)

    embedded = jnp.dot(normal_pool, w_kernel, precision=lax.Precision.HIGHEST)
    device_pos = lax.axis_index("enc") * region_count + lax.axis_index("region")
    own_weights = region_weights(device_pos * reg_dev + jnp.arange(reg_dev, dtype=jnp.int32))
    piece = lax.all_gather(embedded, ("enc", "region"), axis=0, tiled=True)
    piece_ids = jnp.arange(piece.shape[0], dtype=jnp.int32)
    weighted = gaussian(embedded, piece) * region_weights(piece_ids)[None, :]
    kernel_sums = jnp.sum(weighted, axis=1)
    moments = jnp.dot(weighted, piece, precision=lax.Precision.HIGHEST)
    stat_part = region_total * jnp.sum(own_weights * kernel_sums)
    grad_embedded = (
        -2.0
        * region_total
        / embedded.shape[1]
        * own_weights[:, None]
        * (kernel_sums[:, None] * embedded - moments)
    )
    grad_part = GRAD_SCALE * jnp.dot(normal_pool.T, grad_embedded, precision=lax.Precision.HIGHEST)
    statistic, kernel_grad = lax.psum((stat_part, grad_part), ("enc", "region"))
    return (features, statistic, kernel_grad)


def solution(mesh):
    return jax.shard_map(
        local,
        mesh=mesh,
        in_specs=(
            P(("enc", "region"), None),
            P(("enc", "region")),
            P(),
            P(),
            P(),
            P(),
            P(),
            P(),
            P(),
            P(),
            P(("enc", "region")),
            P(),
            P(),
        ),
        out_specs=(P(("enc", "region"), None), P(), P()),
        check_vma=False,
    )
```

profile of v0, /device:TPU:1, one launch (start us, length us, event | category | flops | bytes accessed | tf_op | source)
XLA Modules:
  0.0 473.5 jit_solution(16803794036345877216)
XLA Ops:
  7.2 5.2 %sort.31 = (s32[1024]{0:T(1024)}, s32[1024]{0:T(1024)S(1)}) sort(s32[1024]{0:T(1024)} %param.14, s32[1024]{0:T(1024)S(1)} %iota.81), dimensions={0}, to_apply=%region_0.0 | sort | flops 10240 | bytes 16384 | tf_op jit(solution)/shard_map/jit(argsort)/sort | solution.py:147
  12.4 5.7 %gather_fusion.1 = s32[1024]{0:T(1024)S(1)} fusion(s32[1024]{0:T(1024)} %param.14, s32[1024]{0:T(1024)S(1)} %fusion.90), kind=kCustom, calls=%fused_computation.1 | custom fusion | bytes 12288 | tf_op jit(solution)/shard_map/gather | solution.py:148
  18.9 11.5 %all-to-all-start.1 = ((s32[128,1,8]{2,1,0:T(1,128)}), s32[128,1,8]{2,1,0:T(1,128)S(1)}, u32[]{:S(2)}, u32[]{:S(2)}) async-start(s32[128,1,8]{2,1,0:T(1,128)} %bitcast.2), calls=%async_computation.1 | async-start | bytes 131072 | tf_op jit(solution)/shard_map/all_to_all | solution.py:159
  37.4 5.6 %gather_fusion = bf16[1024,1536]{1,0:T(8,128)(2,1)} fusion(bf16[1024,1536]{1,0:T(8,128)(2,1)S(1)} %copy-done, s32[1024]{0:T(1024)S(1)} %fusion.90), kind=kCustom, calls=%fused_computation | custom fusion | bytes 6295552 | tf_op jit(solution)/shard_map/gather | solution.py:149
  52.1 9.8 %all-to-all-start = ((bf16[128,8,1536]{2,1,0:T(8,128)(2,1)}), bf16[128,8,1536]{2,1,0:T(8,128)(2,1)S(1)}, u32[]{:S(2)}, u32[]{:S(2)}) async-start(bf16[128,8,1536]{2,1,0:T(8,128)(2,1)} %bitcast.105), calls=%async_computation | async-start | bytes 6291456 | tf_op jit(solution)/shard_map/all_to_all | solution.py:152
  69.5 4.4 sort.32
  73.9 29.5 %all-to-all-done = bf16[128,8,1536]{2,1,0:T(8,128)(2,1)S(1)} async-done(((bf16[128,8,1536]{2,1,0:T(8,128)(2,1)}), bf16[128,8,1536]{2,1,0:T(8,128)(2,1)S(1)}, u32[]{:S(2)}, u32[]{:S(2)}) %all-to-all-start) | async-done | bytes 3145760 | tf_op jit(solution)/shard_map/all_to_all | solution.py:152
  103.4 5.6 %gather_fusion.2 = bf16[1024,1536]{1,0:T(8,128)(2,1)} fusion(bf16[1024,1536]{1,0:T(8,128)(2,1)S(1)} %bitcast.104, s32[1024]{0:T(1024)S(1)} %fusion.91), kind=kCustom, calls=%fused_computation.2 | custom fusion | bytes 6295552 | tf_op jit(solution)/shard_map/gather | solution.py:168
  109.0 5.4 %convert_reduce_fusion = (f32[1024]{0:T(1024)S(1)}, bf16[1024,768]{1,0:T(8,128)(2,1)S(1)}) fusion(bf16[1024,1536]{1,0:T(8,128)(2,1)} %gather_fusion.2, bf16[1536,768]{1,0:T(8,128)(2,1)} %param.15), kind=kOutput, calls=%fused_computation.24 | convolution fusion | flops 2418277376 | bytes 7081984 | tf_op jit(solution)/shard_map/dot_general | solution.py:169
  117.8 3.1 collective-permute-start.3
  134.3 3.1 reshape.336
  147.6 22.4 %fusion.121 = (f32[2,8,512]{2,1,0:T(8,128)S(1)}, f32[2,8,512,1024]{3,2,1,0:T(8,128)}) fusion(bf16[2,1024,8,48]{1,3,2,0:T(8,128)(2,1)} %bitcast.109, pred[2,512,1024]{2,1,0:T(8,128)(4,1)} %and_and_fusion, bf16[2,512,8,48]{1,0,3,2:T(2,128)(2,1)} %reshape.331), kind=kOutput, calls=%fused_computation.160 | convolution fusion | flops 847250432 | bytes 36995072 | tf_op jit(solution)/shard_map/sub | solution.py:53
  169.9 13.5 %fusion.56 = bf16[2,512,8,48]{1,3,2,0:T(8,128)(2,1)S(1)} fusion(bf16[2,1024,8,48]{1,3,2,0:T(8,128)(2,1)S(1)} %bitcast.108, f32[2,8,512,1024]{3,2,1,0:T(8,128)} %get-tuple-element.30, f32[2,8,512]{2,1,0:T(8,128)S(1)} %get-tuple-element.29), kind=kOutput, calls=%fused_computation.67 | convolution fusion | flops 822476800 | bytes 35946496 | tf_op jit(solution)/shard_map/bhqk,bkhe->bqhe/dot_general | solution.py:56
  189.5 4.3 copy.68
  193.8 9.3 %reshape_squeeze.7 = bf16[768,4,8,48]{3,2,1,0:T(8,128)(2,1)} reshape(bf16[1,3072,384]{2,1,0:T(8,128)(2,1)} %copy.68) | data formatting | bytes 4718592 | tf_op jit(solution)/shard_map/reshape;squeeze | solution.py:94
  203.1 7.9 %copy.69 = bf16[768,4,8,48]{0,3,2,1:T(8,128)(2,1)} copy(bf16[768,4,8,48]{3,2,1,0:T(8,128)(2,1)} %reshape_squeeze.7) | data formatting | bytes 4718592 | tf_op jit(solution)/shard_map/reshape;squeeze | solution.py:94
  213.6 9.3 %reshape_squeeze.6 = bf16[768,4,8,48]{3,2,1,0:T(8,128)(2,1)} reshape(bf16[1,3072,384]{2,1,0:T(8,128)(2,1)} %copy.64) | data formatting | bytes 4718592 | tf_op jit(solution)/shard_map/reshape;squeeze | solution.py:97
  222.9 8.1 %copy.65 = bf16[768,4,8,48]{0,3,2,1:T(8,128)(2,1)} copy(bf16[768,4,8,48]{3,2,1,0:T(8,128)(2,1)} %reshape_squeeze.6) | data formatting | bytes 4718592 | tf_op jit(solution)/shard_map/reshape;squeeze | solution.py:97
  230.9 16.9 %fusion.112 = (f32[4,8,256]{2,1,0:T(8,128)S(1)}, f32[4,8,256,768]{3,2,1,0:T(8,128)}) fusion(pred[4,256,768]{2,1,0:T(8,128)(4,1)S(1)} %copy-done.9, bf16[768,4,8,48]{0,3,2,1:T(8,128)(2,1)S(1)} %copy-done.5, bf16[256,4,8,48]{0,3,2,1:T(8,128)(2,1)} %copy.67), kind=kOutput, calls=%fused_computation.159 | convolution fusion | flops 635437824 | bytes 29130752 | tf_op jit(solution)/shard_map/sub | solution.py:53
  247.9 11.4 %fusion.53 = bf16[256,4,8,48]{0,3,2,1:T(8,128)(2,1)S(1)} fusion(f32[4,8,256,768]{3,2,1,0:T(8,128)} %get-tuple-element.28, f32[4,8,256]{2,1,0:T(8,128)S(1)} %get-tuple-element.27, bf16[768,4,8,48]{0,3,2,1:T(8,128)(2,1)} %copy.65), kind=kOutput, calls=%fused_computation.65 | convolution fusion | flops 616955904 | bytes 28344320 | tf_op jit(solution)/shard_map/bhqk,bkhe->bqhe/dot_general | solution.py:56
  264.9 3.7 fusion.19
  271.1 40.2 %all-gather = f32[128,4,256]{2,1,0:T(4,128)} all-gather(f32[1,4,256]{2,1,0:T(4,128)S(1)} %bitcast.115), channel_id=1, replica_groups=mesh['enc'=4,'region'=32] {'enc','region'}, dimensions={0}, use_global_device_ids=true | all-gather | bytes 528384 | tf_op jit(solution)/shard_map/all_gather | solution.py:228
  320.6 64.7 %psum.14 = f32[]{:T(128)} all-reduce(f32[]{:T(128)S(6)} %mul.163), channel_id=1, replica_groups=mesh['enc'=4,'region'=32] {'enc','region'}, use_global_device_ids=true, to_apply=%region_24.25 | all-reduce | flops 1 | bytes 8 | tf_op jit(solution)/shard_map/psum | solution.py:242
  385.3 78.8 %all-reduce.2.cloned.1.call-done = f32[768,256]{1,0:T(8,128)} async-done(((f32[768,256]{1,0:T(8,128)}), f32[768,256]{1,0:T(8,128)}) %all-reduce.2.cloned.1.call-update) | async-done | bytes 786448 | tf_op jit(solution)/shard_map/psum | solution.py:242
  (137 shorter events, 77.8 us)
Async XLA Ops:
  7.2 30.2 %copy-start = (bf16[1024,1536]{1,0:T(8,128)(2,1)S(1)}, bf16[1024,1536]{1,0:T(8,128)(2,1)}, u32[]{:S(2)}) copy-start(bf16[1024,1536]{1,0:T(8,128)(2,1)} %param.13) | copy-start | bytes 9437188
  18.1 17.2 %copy-start.19 = (s32[4]{0:T(128)S(1)}, s32[4]{0:T(128)}, u32[]{:S(2)}) copy-start(s32[4]{0:T(128)} %param.24) | copy-start | bytes 52
  18.9 33.2 %all-to-all-start.1 = ((s32[128,1,8]{2,1,0:T(1,128)}), s32[128,1,8]{2,1,0:T(1,128)S(1)}, u32[]{:S(2)}, u32[]{:S(2)}) async-start(s32[128,1,8]{2,1,0:T(1,128)} %bitcast.2), calls=%async_computation.1 | async-start | bytes 131072 | tf_op jit(solution)/shard_map/all_to_all | solution.py:159
  37.4 10.1 %copy-start.18 = (bf16[768]{0:T(1024)(128)(2,1)S(1)}, bf16[768]{0:T(1024)(128)(2,1)}, u32[]{:S(2)}) copy-start(bf16[768]{0:T(1024)(128)(2,1)} %param.16) | copy-start | bytes 4612
  43.0 6.7 %copy-start.4 = (bf16[768,384]{1,0:T(8,128)(2,1)S(1)}, bf16[768,384]{1,0:T(8,128)(2,1)}, u32[]{:S(2)}) copy-start(bf16[768,384]{1,0:T(8,128)(2,1)} %get-tuple-element.17) | copy-start | bytes 1769476
  43.0 8.4 %copy-start.17 = (s32[1024]{0:T(1024)S(1)}, s32[1024]{0:T(1024)}, u32[]{:S(2)}) copy-start(s32[1024]{0:T(1024)} %param.23) | copy-start | bytes 12292
  52.1 51.3 %all-to-all-start = ((bf16[128,8,1536]{2,1,0:T(8,128)(2,1)}), bf16[128,8,1536]{2,1,0:T(8,128)(2,1)S(1)}, u32[]{:S(2)}, u32[]{:S(2)}) async-start(bf16[128,8,1536]{2,1,0:T(8,128)(2,1)} %bitcast.105), calls=%async_computation | async-start | bytes 6291456 | tf_op jit(solution)/shard_map/all_to_all | solution.py:152
  61.9 402.2 %all-reduce.2.cloned.1.call-start = ((), (), s32[]{:S(2)}) async-start(), calls=%async_computation.2 | async-start | bytes 1572864 | tf_op jit(solution)/shard_map/psum | solution.py:242
  109.0 6.0 %copy-start.13 = (bf16[768,384]{0,1:T(8,128)(2,1)S(1)}, bf16[768,384]{0,1:T(8,128)(2,1)}, u32[]{:S(2)}) copy-start(bf16[768,384]{0,1:T(8,128)(2,1)} %copy.77) | copy-start | bytes 1769476
  109.0 6.0 %copy-start.14 = (bf16[768,384]{0,1:T(8,128)(2,1)S(1)}, bf16[768,384]{0,1:T(8,128)(2,1)}, u32[]{:S(2)}) copy-start(bf16[768,384]{0,1:T(8,128)(2,1)} %copy.76) | copy-start | bytes 1769476
  114.4 17.2 %copy-start.6 = (bf16[1024,768]{1,0:T(8,128)(2,1)}, bf16[1024,768]{1,0:T(8,128)(2,1)S(1)}, u32[]{:S(2)}) copy-start(bf16[1024,768]{1,0:T(8,128)(2,1)S(1)} %get-tuple-element.26) | copy-start | bytes 4718596
  115.0 8.3 %copy-start.11 = (bf16[768,384]{0,1:T(8,128)(2,1)S(1)}, bf16[768,384]{0,1:T(8,128)(2,1)}, u32[]{:S(2)}) copy-start(bf16[768,384]{0,1:T(8,128)(2,1)} %copy.75) | copy-start | bytes 1769476
  115.1 8.3 %copy-start.12 = (bf16[768,384]{0,1:T(8,128)(2,1)S(1)}, bf16[768,384]{0,1:T(8,128)(2,1)}, u32[]{:S(2)}) copy-start(bf16[768,384]{0,1:T(8,128)(2,1)} %copy.74) | copy-start | bytes 1769476
  117.8 67.5 %collective-permute-start.3 = (bf16[2,1024,384]{1,2,0:T(8,128)(2,1)}, bf16[2,1024,384]{1,2,0:T(8,128)(2,1)}, u32[]{:S(2)}, u32[]{:S(2)}) collective-permute-start(bf16[2,1024,384]{1,2,0:T(8,128)(2,1)} %fusion.46), channel_id=1, source_target_pairs={{1,0},{2,1},{3,2},{4,3},{5,4},{6,5},{7,6},{8,7},{9,8},{10,9},{11,1... | collective-permute-start | bytes 4718600 | tf_op jit(solution)/shard_map/ppermute | solution.py:22
  120.9 64.4 %collective-permute-start.2 = (bf16[2,1024,384]{1,2,0:T(8,128)(2,1)}, bf16[2,1024,384]{1,2,0:T(8,128)(2,1)}, u32[]{:S(2)}, u32[]{:S(2)}) collective-permute-start(bf16[2,1024,384]{1,2,0:T(8,128)(2,1)} %fusion.46), channel_id=1, source_target_pairs={{0,1},{1,2},{2,3},{3,4},{4,5},{5,6},{6,7},{7,8},{8,9},{9,10},{10,1... | collective-permute-start | bytes 4718600 | tf_op jit(solution)/shard_map/ppermute | solution.py:21
  123.4 8.3 %copy-start.21 = (bf16[768,768]{1,0:T(8,128)(2,1)S(1)}, bf16[768,768]{1,0:T(8,128)(2,1)}, u32[]{:S(2)}) copy-start(bf16[768,768]{1,0:T(8,128)(2,1)} %param.17) | copy-start | bytes 3538948
  125.0 8.2 %copy-start.2 = (bf16[2,1024,384]{1,2,0:T(8,128)(2,1)}, bf16[2,1024,384]{1,2,0:T(8,128)(2,1)S(1)}, u32[]{:S(2)}) copy-start(bf16[2,1024,384]{1,2,0:T(8,128)(2,1)S(1)} %fusion.43) | copy-start | bytes 4718596
  125.9 18.2 %collective-permute-start.1 = (bf16[2,256,384]{1,2,0:T(8,128)(2,1)}, bf16[2,256,384]{1,2,0:T(8,128)(2,1)}, u32[]{:S(2)}, u32[]{:S(2)}) collective-permute-start(bf16[2,256,384]{1,2,0:T(8,128)(2,1)} %get-tuple-element.16), channel_id=1, source_target_pairs={{1,0},{2,1},{3,2},{4,3},{5,4},{6,5},{7,6},{8,7},{9,8},{10,9},{11,1... | collective-permute-start | bytes 1179656 | tf_op jit(solution)/shard_map/ppermute | solution.py:22
  128.9 16.2 %collective-permute-start = (bf16[2,256,384]{1,2,0:T(8,128)(2,1)S(1)}, bf16[2,256,384]{1,2,0:T(8,128)(2,1)}, u32[]{:S(2)}, u32[]{:S(2)}) collective-permute-start(bf16[2,256,384]{1,2,0:T(8,128)(2,1)S(1)} %get-tuple-element.15), channel_id=1, source_target_pairs={{0,1},{1,2},{2,3},{3,4},{4,5},{5,6},{6,7},{7,8},{8,9},{9,10},{10,1... | collective-permute-start | bytes 1179656 | tf_op jit(solution)/shard_map/ppermute | solution.py:21
  222.8 8.1 %copy-start.5 = (bf16[768,4,8,48]{0,3,2,1:T(8,128)(2,1)S(1)}, bf16[768,4,8,48]{0,3,2,1:T(8,128)(2,1)}, u32[]{:S(2)}) copy-start(bf16[768,4,8,48]{0,3,2,1:T(8,128)(2,1)} %copy.69) | copy-start | bytes 7077892
  222.9 8.1 %copy-start.9 = (pred[4,256,768]{2,1,0:T(8,128)(4,1)S(1)}, pred[4,256,768]{2,1,0:T(8,128)(4,1)}, u32[]{:S(2)}) copy-start(pred[4,256,768]{2,1,0:T(8,128)(4,1)} %and_and_fusion.1) | copy-start | bytes 2359300
  268.7 45.8 %copy-start.16 = (f32[512]{0:T(512)S(1)}, f32[512]{0:T(512)}, u32[]{:S(2)}) copy-start(f32[512]{0:T(512)} %compare_select_fusion.2) | copy-start | bytes 6148
  268.7 47.5 %copy-start.20 = (s32[4]{0:T(128)S(1)}, s32[4]{0:T(128)}, u32[]{:S(2)}) copy-start(s32[4]{0:T(128)} %select_reduce_fusion.1) | copy-start | bytes 52
  271.1 195.1 %copy-start.1 = (bf16[1024,1536]{1,0:T(8,128)(2,1)S(1)}, bf16[1024,1536]{1,0:T(8,128)(2,1)}, u32[]{:S(2)}) copy-start(bf16[1024,1536]{1,0:T(8,128)(2,1)} %param.13) | copy-start | bytes 9437188
  (5 other events, 19.3 us)
Sparse Core Ops, SparseCore 0:
  320.1 143.9 all-reduce.1
where the time goes:
time: 479 us; the launch traced here: 473 us
  waiting for transfers between devices  112 us (23%)
  blocking collectives  105 us (22%)
  local copies, waits for them, and re-layouts  96.9 us (20%)
  matrix products  84.8 us (18%)
  starting transfers between devices  33.1 us (7%)
  other arithmetic  25.6 us (5%)
  between operations  16.5 us (3%)
    psum x1, waiting for transfers between devices, local(): statistic, kernel_grad = lax.psum((stat_part, grad_part), ('enc', 'region'))  78.8 us
    psum x1, blocking collectives, local(): statistic, kernel_grad = lax.psum((stat_part, grad_part), ('enc', 'region'))  64.7 us
    all_gather x1, blocking collectives, local(): piece = lax.all_gather(embedded, ('enc', 'region'), axis=0, tiled=True)  40.2 us
    sub x2, matrix products, attend(): exponent = jnp.where(allowed, jnp.exp(masked - row_peak), 0.0)  39.3 us
    all_to_all x1, waiting for transfers between devices, local(): lax.all_to_all(payload.reshape(senders, per_peer, width_sent), ('enc', 'r...  29.5 us
    dot_general x2, matrix products, attend(): jnp.einsum('bhqk,bkhe->bqhe', weights, values, preferred_element_type=jnp...  24.8 us
    another operation x2, local copies, waits for them, and re-layouts, block_context(): far_kv[1].reshape(3 * group_rows, DILATION, head_count, head_size)  17.4 us
    another operation x2, local copies, waits for them, and re-layouts, block_context(): far_kv[0].reshape(3 * group_rows, DILATION, head_count, head_size)  17.2 us
  transfers between devices with their start and end apart: 7, of which 4 were waited for; matrix products, arithmetic and copies ran while one was open for 18% of the time, Pallas kernels for 0%

commit v1 on v0

--- a/solution.py
+++ b/solution.py
@@ -225,7 +225,19 @@
     embedded = jnp.dot(normal_pool, w_kernel, precision=lax.Precision.HIGHEST)
     device_pos = lax.axis_index("enc") * region_count + lax.axis_index("region")
     own_weights = region_weights(device_pos * reg_dev + jnp.arange(reg_dev, dtype=jnp.int32))
-    piece = lax.all_gather(embedded, ("enc", "region"), axis=0, tiled=True)
+
+    def feed_the_frame(tile_in, named_axis):
+        return jnp.concatenate(
+            lax.all_to_all(
+                jnp.stack([tile_in] * lax.axis_size(named_axis)),
+                named_axis,
+                split_axis=0,
+                concat_axis=0,
+            ),
+            0,
+        )
+
+    piece = feed_the_frame(embedded, ("enc", "region"))
     piece_ids = jnp.arange(piece.shape[0], dtype=jnp.int32)
     weighted = gaussian(embedded, piece) * region_weights(piece_ids)[None, :]
     kernel_sums = jnp.sum(weighted, axis=1)

time: 479 us -> 461 us (0.962)
  blocking collectives: 105 us -> 62.6 us
  waiting for transfers between devices: 112 us -> 127 us
  starting transfers between devices: 33.1 us -> 41.5 us
    all_gather x1 -> x0, blocking collectives: 40.2 us -> none  [local(): piece = lax.all_gather(embedded, ('enc', 'region'), axis=0, tiled=True)]
    all_to_all x0 -> x1, waiting for transfers between devices: none -> 13 us  [feed_the_frame(): lax.all_to_all(jnp.stack([tile_in] * lax.axis_size(named_axis)), named_ax...]
    all_to_all x0 -> x1, starting transfers between devices: none -> 8.31 us  [feed_the_frame(): lax.all_to_all(jnp.stack([tile_in] * lax.axis_size(named_axis)), named_ax...]
    unnamed x51 -> x50, local copies, waits for them, and re-layouts: 13.8 us -> 11.8 us
  transfers between devices with their start and end apart: 7 -> 8, of which waited for: 4 -> 5; matrix products, arithmetic and copies ran while one was open for 18% -> 19% of each run, Pallas kernels for 0% -> 0%
where the time goes in v1:
time: 461 us; the launch traced here: 455 us
  waiting for transfers between devices  127 us (28%)
  local copies, waits for them, and re-layouts  98 us (21%)
  matrix products  84.8 us (18%)
  blocking collectives  62.6 us (14%)
  starting transfers between devices  41.5 us (9%)
  other arithmetic  25.1 us (5%)
  between operations  16.4 us (4%)
    psum x1, waiting for transfers between devices, local(): statistic, kernel_grad = lax.psum((stat_part, grad_part), ('enc', 'region'))  79.6 us
    psum x1, blocking collectives, local(): statistic, kernel_grad = lax.psum((stat_part, grad_part), ('enc', 'region'))  62.6 us
    sub x2, matrix products, attend(): exponent = jnp.where(allowed, jnp.exp(masked - row_peak), 0.0)  39.3 us
    all_to_all x1, waiting for transfers between devices, local(): lax.all_to_all(payload.reshape(senders, per_peer, width_sent), ('enc', 'r...  30.6 us
    dot_general x2, matrix products, attend(): jnp.einsum('bhqk,bkhe->bqhe', weights, values, preferred_element_type=jnp...  24.8 us
    another operation x2, local copies, waits for them, and re-layouts, block_context(): far_kv[1].reshape(3 * group_rows, DILATION, head_count, head_size)  17.4 us
    another operation x2, local copies, waits for them, and re-layouts, block_context(): far_kv[0].reshape(3 * group_rows, DILATION, head_count, head_size)  17.2 us
    all_to_all x1, waiting for transfers between devices, feed_the_frame(): lax.all_to_all(jnp.stack([tile_in] * lax.axis_size(named_axis)), named_ax...  13 us
  transfers between devices with their start and end apart: 8, of which 5 were waited for; matrix products, arithmetic and copies ran while one was open for 19% of the time, Pallas kernels for 0%

profile of v1, /device:TPU:1, one launch (start us, length us, event | category | flops | bytes accessed | tf_op | source)
XLA Modules:
  0.0 455.2 jit_solution(452687411190350283)
XLA Ops:
  7.2 5.2 %sort.31 = (s32[1024]{0:T(1024)}, s32[1024]{0:T(1024)S(1)}) sort(s32[1024]{0:T(1024)} %param.14, s32[1024]{0:T(1024)S(1)} %iota.81), dimensions={0}, to_apply=%region_0.0 | sort | flops 10240 | bytes 16384 | tf_op jit(solution)/shard_map/jit(argsort)/sort | solution.py:147
  12.4 5.7 %gather_fusion.1 = s32[1024]{0:T(1024)S(1)} fusion(s32[1024]{0:T(1024)} %param.14, s32[1024]{0:T(1024)S(1)} %fusion.91), kind=kCustom, calls=%fused_computation.1 | custom fusion | bytes 12288 | tf_op jit(solution)/shard_map/gather | solution.py:148
  18.8 11.5 %all-to-all-start.1 = ((s32[128,1,8]{2,1,0:T(1,128)}), s32[128,1,8]{2,1,0:T(1,128)S(1)}, u32[]{:S(2)}, u32[]{:S(2)}) async-start(s32[128,1,8]{2,1,0:T(1,128)} %bitcast.2), calls=%async_computation.1 | async-start | bytes 131072 | tf_op jit(solution)/shard_map/all_to_all | solution.py:159
  36.5 5.6 %gather_fusion = bf16[1024,1536]{1,0:T(8,128)(2,1)} fusion(bf16[1024,1536]{1,0:T(8,128)(2,1)S(1)} %copy-done, s32[1024]{0:T(1024)S(1)} %fusion.91), kind=kCustom, calls=%fused_computation | custom fusion | bytes 6295552 | tf_op jit(solution)/shard_map/gather | solution.py:149
  51.9 10.4 %all-to-all-start = ((bf16[128,8,1536]{2,1,0:T(8,128)(2,1)}), bf16[128,8,1536]{2,1,0:T(8,128)(2,1)S(1)}, u32[]{:S(2)}, u32[]{:S(2)}) async-start(bf16[128,8,1536]{2,1,0:T(8,128)(2,1)} %bitcast.104), calls=%async_computation | async-start | bytes 6291456 | tf_op jit(solution)/shard_map/all_to_all | solution.py:152
  68.8 4.4 sort.32
  73.2 30.6 %all-to-all-done = bf16[128,8,1536]{2,1,0:T(8,128)(2,1)S(1)} async-done(((bf16[128,8,1536]{2,1,0:T(8,128)(2,1)}), bf16[128,8,1536]{2,1,0:T(8,128)(2,1)S(1)}, u32[]{:S(2)}, u32[]{:S(2)}) %all-to-all-start) | async-done | bytes 3145760 | tf_op jit(solution)/shard_map/all_to_all | solution.py:152
  103.7 5.6 %gather_fusion.2 = bf16[1024,1536]{1,0:T(8,128)(2,1)} fusion(bf16[1024,1536]{1,0:T(8,128)(2,1)S(1)} %bitcast.103, s32[1024]{0:T(1024)S(1)} %fusion.92), kind=kCustom, calls=%fused_computation.2 | custom fusion | bytes 6295552 | tf_op jit(solution)/shard_map/gather | solution.py:168
  109.3 5.4 %convert_reduce_fusion = (f32[1024]{0:T(1024)S(1)}, bf16[1024,768]{1,0:T(8,128)(2,1)S(1)}) fusion(bf16[1024,1536]{1,0:T(8,128)(2,1)} %gather_fusion.2, bf16[1536,768]{1,0:T(8,128)(2,1)} %param.15), kind=kOutput, calls=%fused_computation.24 | convolution fusion | flops 2418277376 | bytes 7081984 | tf_op jit(solution)/shard_map/dot_general | solution.py:169
  134.6 3.1 reshape.343
  147.9 22.4 %fusion.122 = (f32[2,8,512]{2,1,0:T(8,128)S(1)}, f32[2,8,512,1024]{3,2,1,0:T(8,128)}) fusion(bf16[2,1024,8,48]{1,3,2,0:T(8,128)(2,1)} %bitcast.108, pred[2,512,1024]{2,1,0:T(8,128)(4,1)} %and_and_fusion, bf16[2,512,8,48]{1,0,3,2:T(2,128)(2,1)} %reshape.338), kind=kOutput, calls=%fused_computation.161 | convolution fusion | flops 847250432 | bytes 36995072 | tf_op jit(solution)/shard_map/sub | solution.py:53
  170.2 13.5 %fusion.56 = bf16[2,512,8,48]{1,3,2,0:T(8,128)(2,1)S(1)} fusion(bf16[2,1024,8,48]{1,3,2,0:T(8,128)(2,1)S(1)} %bitcast.107, f32[2,8,512,1024]{3,2,1,0:T(8,128)} %get-tuple-element.30, f32[2,8,512]{2,1,0:T(8,128)S(1)} %get-tuple-element.29), kind=kOutput, calls=%fused_computation.67 | convolution fusion | flops 822476800 | bytes 35946496 | tf_op jit(solution)/shard_map/bhqk,bkhe->bqhe/dot_general | solution.py:56
  189.8 4.3 copy.121
  194.1 9.3 %reshape_squeeze.7 = bf16[768,4,8,48]{3,2,1,0:T(8,128)(2,1)} reshape(bf16[1,3072,384]{2,1,0:T(8,128)(2,1)} %copy.121) | data formatting | bytes 4718592 | tf_op jit(solution)/shard_map/reshape;squeeze | solution.py:94
  203.4 7.9 %copy.122 = bf16[768,4,8,48]{0,3,2,1:T(8,128)(2,1)} copy(bf16[768,4,8,48]{3,2,1,0:T(8,128)(2,1)} %reshape_squeeze.7) | data formatting | bytes 4718592 | tf_op jit(solution)/shard_map/reshape;squeeze | solution.py:94
  213.9 9.3 %reshape_squeeze.6 = bf16[768,4,8,48]{3,2,1,0:T(8,128)(2,1)} reshape(bf16[1,3072,384]{2,1,0:T(8,128)(2,1)} %copy.117) | data formatting | bytes 4718592 | tf_op jit(solution)/shard_map/reshape;squeeze | solution.py:97
  223.2 8.1 %copy.118 = bf16[768,4,8,48]{0,3,2,1:T(8,128)(2,1)} copy(bf16[768,4,8,48]{3,2,1,0:T(8,128)(2,1)} %reshape_squeeze.6) | data formatting | bytes 4718592 | tf_op jit(solution)/shard_map/reshape;squeeze | solution.py:97
  231.3 16.9 %fusion.113 = (f32[4,8,256]{2,1,0:T(8,128)S(1)}, f32[4,8,256,768]{3,2,1,0:T(8,128)}) fusion(pred[4,256,768]{2,1,0:T(8,128)(4,1)S(1)} %copy-done.9, bf16[768,4,8,48]{0,3,2,1:T(8,128)(2,1)S(1)} %copy-done.5, bf16[256,4,8,48]{0,3,2,1:T(8,128)(2,1)} %copy.120), kind=kOutput, calls=%fused_computation.160 | convolution fusion | flops 635437824 | bytes 29130752 | tf_op jit(solution)/shard_map/sub | solution.py:53
  248.2 11.4 %fusion.53 = bf16[256,4,8,48]{0,3,2,1:T(8,128)(2,1)S(1)} fusion(f32[4,8,256,768]{3,2,1,0:T(8,128)} %get-tuple-element.28, f32[4,8,256]{2,1,0:T(8,128)S(1)} %get-tuple-element.27, bf16[768,4,8,48]{0,3,2,1:T(8,128)(2,1)} %copy.118), kind=kOutput, calls=%fused_computation.65 | convolution fusion | flops 616955904 | bytes 28344320 | tf_op jit(solution)/shard_map/bhqk,bkhe->bqhe/dot_general | solution.py:56
  265.3 3.7 fusion.19
  272.2 8.3 %all-to-all-start.2 = ((f32[128,4,256]{2,1,0:T(4,128)}), f32[128,4,256]{2,1,0:T(4,128)}, u32[]{:S(2)}, u32[]{:S(2)}) async-start(f32[128,4,256]{2,1,0:T(4,128)} %stack.29), calls=%async_computation.2 | async-start | bytes 1048576 | tf_op jit(solution)/shard_map/all_to_all | solution.py:231
  280.9 13.0 %all-to-all-done.2 = f32[128,4,256]{2,1,0:T(4,128)} async-done(((f32[128,4,256]{2,1,0:T(4,128)}), f32[128,4,256]{2,1,0:T(4,128)}, u32[]{:S(2)}, u32[]{:S(2)}) %all-to-all-start.2) | async-done | bytes 524320 | tf_op jit(solution)/shard_map/all_to_all | solution.py:231
  303.5 62.6 %psum.14 = f32[]{:T(128)} all-reduce(f32[]{:T(128)S(6)} %mul.164), channel_id=1, replica_groups=mesh['enc'=4,'region'=32] {'enc','region'}, use_global_device_ids=true, to_apply=%region_24.25 | all-reduce | flops 1 | bytes 8 | tf_op jit(solution)/shard_map/psum | solution.py:254
  366.1 79.6 %all-reduce.2.cloned.1.call-done = f32[768,256]{1,0:T(8,128)} async-done(((f32[768,256]{1,0:T(8,128)}), f32[768,256]{1,0:T(8,128)}) %all-reduce.2.cloned.1.call-update) | async-done | bytes 786448 | tf_op jit(solution)/shard_map/psum | solution.py:254
  (141 shorter events, 81.0 us)
Async XLA Ops:
  7.2 29.3 %copy-start = (bf16[1024,1536]{1,0:T(8,128)(2,1)S(1)}, bf16[1024,1536]{1,0:T(8,128)(2,1)}, u32[]{:S(2)}) copy-start(bf16[1024,1536]{1,0:T(8,128)(2,1)} %param.13) | copy-start | bytes 9437188
  18.8 33.0 %all-to-all-start.1 = ((s32[128,1,8]{2,1,0:T(1,128)}), s32[128,1,8]{2,1,0:T(1,128)S(1)}, u32[]{:S(2)}, u32[]{:S(2)}) async-start(s32[128,1,8]{2,1,0:T(1,128)} %bitcast.2), calls=%async_computation.1 | async-start | bytes 131072 | tf_op jit(solution)/shard_map/all_to_all | solution.py:159
  36.5 10.1 %copy-start.18 = (bf16[768]{0:T(1024)(128)(2,1)S(1)}, bf16[768]{0:T(1024)(128)(2,1)}, u32[]{:S(2)}) copy-start(bf16[768]{0:T(1024)(128)(2,1)} %param.16) | copy-start | bytes 4612
  42.1 6.7 %copy-start.4 = (bf16[768,384]{1,0:T(8,128)(2,1)S(1)}, bf16[768,384]{1,0:T(8,128)(2,1)}, u32[]{:S(2)}) copy-start(bf16[768,384]{1,0:T(8,128)(2,1)} %get-tuple-element.17) | copy-start | bytes 1769476
  42.1 7.8 %copy-start.19 = (s32[4]{0:T(128)S(1)}, s32[4]{0:T(128)}, u32[]{:S(2)}) copy-start(s32[4]{0:T(128)} %param.24) | copy-start | bytes 52
  42.1 9.1 %copy-start.17 = (s32[1024]{0:T(1024)S(1)}, s32[1024]{0:T(1024)}, u32[]{:S(2)}) copy-start(s32[1024]{0:T(1024)} %param.23) | copy-start | bytes 12292
  51.9 51.8 %all-to-all-start = ((bf16[128,8,1536]{2,1,0:T(8,128)(2,1)}), bf16[128,8,1536]{2,1,0:T(8,128)(2,1)S(1)}, u32[]{:S(2)}, u32[]{:S(2)}) async-start(bf16[128,8,1536]{2,1,0:T(8,128)(2,1)} %bitcast.104), calls=%async_computation | async-start | bytes 6291456 | tf_op jit(solution)/shard_map/all_to_all | solution.py:152
  109.3 6.0 %copy-start.14 = (bf16[768,384]{0,1:T(8,128)(2,1)S(1)}, bf16[768,384]{0,1:T(8,128)(2,1)}, u32[]{:S(2)}) copy-start(bf16[768,384]{0,1:T(8,128)(2,1)} %copy.132) | copy-start | bytes 1769476
  114.7 17.2 %copy-start.6 = (bf16[1024,768]{1,0:T(8,128)(2,1)}, bf16[1024,768]{1,0:T(8,128)(2,1)S(1)}, u32[]{:S(2)}) copy-start(bf16[1024,768]{1,0:T(8,128)(2,1)S(1)} %get-tuple-element.26) | copy-start | bytes 4718596
  115.4 8.3 %copy-start.11 = (bf16[768,384]{0,1:T(8,128)(2,1)S(1)}, bf16[768,384]{0,1:T(8,128)(2,1)}, u32[]{:S(2)}) copy-start(bf16[768,384]{0,1:T(8,128)(2,1)} %copy.131) | copy-start | bytes 1769476
  115.4 8.3 %copy-start.12 = (bf16[768,384]{0,1:T(8,128)(2,1)S(1)}, bf16[768,384]{0,1:T(8,128)(2,1)}, u32[]{:S(2)}) copy-start(bf16[768,384]{0,1:T(8,128)(2,1)} %copy.130) | copy-start | bytes 1769476
  118.1 67.5 %collective-permute-start.3 = (bf16[2,1024,384]{1,2,0:T(8,128)(2,1)}, bf16[2,1024,384]{1,2,0:T(8,128)(2,1)}, u32[]{:S(2)}, u32[]{:S(2)}) collective-permute-start(bf16[2,1024,384]{1,2,0:T(8,128)(2,1)} %fusion.46), channel_id=1, source_target_pairs={{1,0},{2,1},{3,2},{4,3},{5,4},{6,5},{7,6},{8,7},{9,8},{10,9},{11,1... | collective-permute-start | bytes 4718600 | tf_op jit(solution)/shard_map/ppermute | solution.py:22
  121.1 64.4 %collective-permute-start.2 = (bf16[2,1024,384]{1,2,0:T(8,128)(2,1)}, bf16[2,1024,384]{1,2,0:T(8,128)(2,1)}, u32[]{:S(2)}, u32[]{:S(2)}) collective-permute-start(bf16[2,1024,384]{1,2,0:T(8,128)(2,1)} %fusion.46), channel_id=1, source_target_pairs={{0,1},{1,2},{2,3},{3,4},{4,5},{5,6},{6,7},{7,8},{8,9},{9,10},{10,1... | collective-permute-start | bytes 4718600 | tf_op jit(solution)/shard_map/ppermute | solution.py:21
  123.7 8.3 %copy-start.21 = (bf16[768,768]{1,0:T(8,128)(2,1)S(1)}, bf16[768,768]{1,0:T(8,128)(2,1)}, u32[]{:S(2)}) copy-start(bf16[768,768]{1,0:T(8,128)(2,1)} %param.17) | copy-start | bytes 3538948
  125.3 8.2 %copy-start.2 = (bf16[2,1024,384]{1,2,0:T(8,128)(2,1)}, bf16[2,1024,384]{1,2,0:T(8,128)(2,1)S(1)}, u32[]{:S(2)}) copy-start(bf16[2,1024,384]{1,2,0:T(8,128)(2,1)S(1)} %fusion.43) | copy-start | bytes 4718596
  126.2 18.2 %collective-permute-start.1 = (bf16[2,256,384]{1,2,0:T(8,128)(2,1)}, bf16[2,256,384]{1,2,0:T(8,128)(2,1)}, u32[]{:S(2)}, u32[]{:S(2)}) collective-permute-start(bf16[2,256,384]{1,2,0:T(8,128)(2,1)} %get-tuple-element.16), channel_id=1, source_target_pairs={{1,0},{2,1},{3,2},{4,3},{5,4},{6,5},{7,6},{8,7},{9,8},{10,9},{11,1... | collective-permute-start | bytes 1179656 | tf_op jit(solution)/shard_map/ppermute | solution.py:22
  129.2 16.2 %collective-permute-start = (bf16[2,256,384]{1,2,0:T(8,128)(2,1)S(1)}, bf16[2,256,384]{1,2,0:T(8,128)(2,1)}, u32[]{:S(2)}, u32[]{:S(2)}) collective-permute-start(bf16[2,256,384]{1,2,0:T(8,128)(2,1)S(1)} %get-tuple-element.15), channel_id=1, source_target_pairs={{0,1},{1,2},{2,3},{3,4},{4,5},{5,6},{6,7},{7,8},{8,9},{9,10},{10,1... | collective-permute-start | bytes 1179656 | tf_op jit(solution)/shard_map/ppermute | solution.py:21
  223.2 8.1 %copy-start.5 = (bf16[768,4,8,48]{0,3,2,1:T(8,128)(2,1)S(1)}, bf16[768,4,8,48]{0,3,2,1:T(8,128)(2,1)}, u32[]{:S(2)}) copy-start(bf16[768,4,8,48]{0,3,2,1:T(8,128)(2,1)} %copy.122) | copy-start | bytes 7077892
  223.2 8.1 %copy-start.9 = (pred[4,256,768]{2,1,0:T(8,128)(4,1)S(1)}, pred[4,256,768]{2,1,0:T(8,128)(4,1)}, u32[]{:S(2)}) copy-start(pred[4,256,768]{2,1,0:T(8,128)(4,1)} %and_and_fusion.1) | copy-start | bytes 2359300
  269.0 11.6 %copy-start.20 = (s32[4]{0:T(128)S(1)}, s32[4]{0:T(128)}, u32[]{:S(2)}) copy-start(s32[4]{0:T(128)} %param.24) | copy-start | bytes 52
  269.0 11.8 %copy-start.16 = (s32[512]{0:T(512)S(1)}, s32[512]{0:T(512)}, u32[]{:S(2)}) copy-start(s32[512]{0:T(512)} %add_select_fusion.1) | copy-start | bytes 6148
  272.2 21.7 %all-to-all-start.2 = ((f32[128,4,256]{2,1,0:T(4,128)}), f32[128,4,256]{2,1,0:T(4,128)}, u32[]{:S(2)}, u32[]{:S(2)}) async-start(f32[128,4,256]{2,1,0:T(4,128)} %stack.29), calls=%async_computation.2 | async-start | bytes 1048576 | tf_op jit(solution)/shard_map/all_to_all | solution.py:231
  280.6 167.3 %copy-start.1 = (bf16[1024,1536]{1,0:T(8,128)(2,1)S(1)}, bf16[1024,1536]{1,0:T(8,128)(2,1)}, u32[]{:S(2)}) copy-start(bf16[1024,1536]{1,0:T(8,128)(2,1)} %param.13) | copy-start | bytes 9437188
  280.6 165.2 %all-reduce.2.cloned.1.call-start = ((), (), s32[]{:S(2)}) async-start(), calls=%async_computation.3 | async-start | bytes 1572864 | tf_op jit(solution)/shard_map/psum | solution.py:254
  (6 other events, 25.4 us)
Sparse Core Ops, SparseCore 0:
  303.0 142.7 all-reduce.1
